TPU v7x, 32 devices: a whole 2x2x4 slice. The times are simulated.
32 devices in a mesh: row: 2 (over y), col: 16 (over z, x, core).
Axes of the slice: x: 2, y: 2, z: 4, core: 2. Of those that a mesh axis runs over, the one named last changes fastest.
Arguments:
- matrix: float32 [16384, 16384], P('row', 'col'), may hold values from -6 to 6
- reflectors: float32 [16384, 256], P(('row', 'col')), may hold values from -0.046875 to 0.046875
- factor: float32 [256, 256], replicated, may hold values from -0.375 to 0.375
Outputs:
- updated: float32 [16384, 16384], P('row', 'col')
- correction: float32 [16384, 256], P(('row', 'col'))
All inputs are finite; a program needn't handle non-finite values.
Results may differ from a plain program's by a relative error of at most 0.000078.
Values sent between devices are 32-bit elements; how exact they have to be, the bound alone decides.
A program may use at most 192 MiB of HBM per device.

v0:
```python
import jax
import jax.numpy as jnp
from jax import lax
from jax.sharding import PartitionSpec as P


def broadcast(value, axis, root):
    mine = lax.axis_index(axis) == root
    return lax.psum(jnp.where(mine, value, jnp.zeros_like(value)), axis)


def mult(left, right):
    return jnp.dot(left, right, precision=lax.Precision.HIGHEST, preferred_element_type=jnp.float32)


def mult_tn(left, right):
    return lax.dot_general(
        left,
        right,
        (((0,), (0,)), ((), ())),
        precision=lax.Precision.HIGHEST,
        preferred_element_type=jnp.float32,
    )


def mult_nt(left, right):
    return lax.dot_general(
        left,
        right,
        (((1,), (1,)), ((), ())),
        precision=lax.Precision.HIGHEST,
        preferred_element_type=jnp.float32,
    )


def correct(local_vectors, image, factor):
    gram_matrix = lax.psum(mult_tn(local_vectors, image), ("row", "col"))
    inner = mult(mult_tn(factor, gram_matrix), factor)
    return mult(image, factor) - 0.5 * mult(local_vectors, inner)


def on_device(matrix, reflectors, factor):
    tile_rows, tile_cols = matrix.shape
    col_ratio = tile_rows // tile_cols
    col_index = lax.axis_index("col")
    owner_index = col_index // col_ratio
    offset_rows = col_index % col_ratio * tile_cols
    vec_rows = lax.all_gather(reflectors, "col", axis=0, tiled=True)
    vec_cols = broadcast(
        lax.dynamic_slice_in_dim(vec_rows, offset_rows, tile_cols, 0), "row", owner_index
    )
    image = lax.psum_scatter(mult(matrix, vec_cols), "col", scatter_dimension=0, tiled=True)
    correction = correct(reflectors, image, factor)
    corr_rows = lax.all_gather(correction, "col", axis=0, tiled=True)
    corr_cols = broadcast(
        lax.dynamic_slice_in_dim(corr_rows, offset_rows, tile_cols, 0), "row", owner_index
    )
    updated = matrix - mult_nt(vec_rows, corr_cols) - mult_nt(corr_rows, vec_cols)
    return (updated, correction)


def solution(mesh):
    placed = (P("row", "col"), P(("row", "col"), None), P())
    return jax.shard_map(
        on_device,
        mesh=mesh,
        in_specs=placed,
        out_specs=(P("row", "col"), P(("row", "col"), None)),
        check_vma=False,
    )
```

profile of v0, /device:TPU:0, one launch (start us, length us, event | category | flops | bytes accessed | tf_op | source)
XLA Modules:
  0.0 628.8 jit_solution(12058716706127054088)
XLA Ops:
  7.2 0.7 all-gather.3.cloned.1.call-update
  7.9 0.0 all-reduce.4.cloned.1.call-start
  8.0 79.8 %all-gather.3.cloned.1.call-done = f32[8192,256]{1,0:T(8,128)} async-done(((f32[512,256]{1,0:T(8,128)}), f32[8192,256]{1,0:T(8,128)}) %all-gather.3.cloned.1.call-update) | async-done | bytes 8388624 | tf_op jit(solution)/shard_map/all_gather | solution.py:48
  87.8 2.3 dynamic-slice_select_fusion.1
  90.1 0.0 reduce-scatter.2.cloned.1.call-start
  90.1 38.9 %all-reduce.4.cloned.1.call-done = f32[1024,256]{1,0:T(8,128)} async-done(((f32[1024,256]{1,0:T(8,128)}), f32[1024,256]{1,0:T(8,128)}) %all-reduce.4.cloned.1.call-update) | async-done | bytes 1048592 | tf_op jit(solution)/shard_map/psum | solution.py:9
  129.0 58.4 %convolution_bitcast_fusion = f32[8192,256]{0,1:T(8,128)} fusion(f32[1024,256]{1,0:T(8,128)} %all-reduce.4.cloned.1.call-done, f32[8192,1024]{1,0:T(8,128)} %param.3), kind=kOutput, calls=%fused_computation.2 | convolution fusion | flops 25769803776 | bytes 42991616 | tf_op jit(solution)/shard_map/dot_general | solution.py:13
  187.5 0.0 all-reduce.6.cloned.1.call-start
  187.5 105.0 %reduce-scatter.2.cloned.1.call-done = f32[512,256]{0,1:T(8,128)} async-done(((f32[8192,256]{0,1:T(8,128)}), f32[512,256]{0,1:T(8,128)}) %reduce-scatter.2.cloned.1.call-update) | async-done | bytes 524304 | tf_op jit(solution)/shard_map/reduce_scatter | solution.py:52
  292.5 2.3 convolution_bitcast_fusion.1
  294.9 0.0 all-gather.5.cloned.1.call-start
  294.9 2.0 fusion.3
  297.0 127.2 %all-reduce.6.cloned.1.call-done = f32[256,256]{0,1:T(8,128)} async-done(((f32[256,256]{0,1:T(8,128)}), f32[256,256]{0,1:T(8,128)}) %all-reduce.6.cloned.1.call-update) | async-done | bytes 262160 | tf_op jit(solution)/shard_map/psum | solution.py:37
  424.1 1.3 fusion.4
  425.5 0.6 fusion.5
  426.1 1.4 fusion.2
  427.5 0.0 all-reduce.8.cloned.1.call-start
  427.5 31.3 %copy.6 = f32[8192,1024]{0,1:T(8,128)} copy(f32[8192,1024]{1,0:T(8,128)} %param.3) | data formatting | bytes 67108864 | tf_op args[0]
  458.8 42.7 %all-gather.5.cloned.1.call-done = f32[8192,256]{1,0:T(8,128)} async-done(((f32[512,256]{1,0:T(8,128)}), f32[8192,256]{1,0:T(8,128)}) %all-gather.5.cloned.1.call-update) | async-done | bytes 8388624 | tf_op jit(solution)/shard_map/all_gather | solution.py:54
  501.6 2.3 dynamic-slice_select_fusion
  503.9 32.1 %fusion.6 = f32[8192,1024]{0,1:T(8,128)} fusion(f32[8192,256]{1,0:T(8,128)} %all-gather.5.cloned.1.call-done, f32[1024,256]{1,0:T(8,128)S(1)} %copy-done.3), kind=kOutput, calls=%fused_computation.12 | convolution fusion | flops 25769803776 | bytes 42991616 | tf_op jit(solution)/shard_map/dot_general | solution.py:27
  536.0 6.3 %all-reduce.8.cloned.1.call-done = f32[1024,256]{1,0:T(8,128)} async-done(((f32[1024,256]{1,0:T(8,128)}), f32[1024,256]{1,0:T(8,128)}) %all-reduce.8.cloned.1.call-update) | async-done | bytes 1048592 | tf_op jit(solution)/shard_map/psum | solution.py:9
  542.3 46.2 %fusion = f32[8192,1024]{0,1:T(8,128)} fusion(f32[8192,1024]{0,1:T(8,128)} %fusion.6, f32[8192,1024]{0,1:T(8,128)} %copy.6, f32[1024,256]{1,0:T(8,128)} %all-reduce.8.cloned.1.call-done, f32[8192,256]{1,0:T(8,128)} %all-gather.3.cloned.1.call-done), kind=kOutput, calls=%fused_computation.1 | convolution fusion | flops 25786580992 | bytes 110100480 | tf_op jit(solution)/shard_map/dot_general | solution.py:27
  588.5 33.4 %copy.8 = f32[8192,1024]{1,0:T(8,128)} copy(f32[8192,1024]{0,1:T(8,128)} %fusion) | data formatting | bytes 67108864
  (14 shorter events, 0.1 us)
Async XLA Ops:
  7.2 287.8 %copy-start = (f32[256,256]{1,0:T(8,128)S(1)}, f32[256,256]{1,0:T(8,128)}, u32[]{:S(2)}) copy-start(f32[256,256]{1,0:T(8,128)} %param.5) | copy-start | bytes 786436
  7.2 285.3 %copy-start.2 = (f32[512,256]{1,0:T(8,128)S(1)}, f32[512,256]{1,0:T(8,128)}, u32[]{:S(2)}) copy-start(f32[512,256]{1,0:T(8,128)} %param.4) | copy-start | bytes 1572868
  7.2 80.6 %all-gather.3.cloned.1.call-start = ((), (), s32[]{:S(2)}) async-start(), calls=%async_computation.1 | async-start | bytes 8912896 | tf_op jit(solution)/shard_map/all_gather | solution.py:48
  7.9 121.1 %all-reduce.4.cloned.1.call-start = ((), (), s32[]{:S(2)}) async-start(), calls=%async_computation.2 | async-start | bytes 2097152 | tf_op jit(solution)/shard_map/psum | solution.py:9
  90.1 202.4 %reduce-scatter.2.cloned.1.call-start = ((), (), s32[]{:S(2)}) async-start(), calls=%async_computation.3 | async-start | bytes 8912896 | tf_op jit(solution)/shard_map/reduce_scatter | solution.py:52
  187.5 236.7 %all-reduce.6.cloned.1.call-start = ((), (), s32[]{:S(2)}) async-start(), calls=%async_computation.4 | async-start | bytes 524288 | tf_op jit(solution)/shard_map/psum | solution.py:37
  294.9 206.7 %all-gather.5.cloned.1.call-start = ((), (), s32[]{:S(2)}) async-start(), calls=%async_computation.5 | async-start | bytes 8912896 | tf_op jit(solution)/shard_map/all_gather | solution.py:54
  427.5 76.4 %copy-start.3 = (f32[1024,256]{1,0:T(8,128)S(1)}, f32[1024,256]{1,0:T(8,128)}, u32[]{:S(2)}) copy-start(f32[1024,256]{1,0:T(8,128)} %all-reduce.4.cloned.1.call-done) | copy-start | bytes 3145732
  427.5 114.8 %all-reduce.8.cloned.1.call-start = ((), (), s32[]{:S(2)}) async-start(), calls=%async_computation.6 | async-start | bytes 2097152 | tf_op jit(solution)/shard_map/psum | solution.py:9
  542.3 79.6 %copy-start.1 = (f32[256,256]{1,0:T(8,128)S(1)}, f32[256,256]{1,0:T(8,128)}, u32[]{:S(2)}) copy-start(f32[256,256]{1,0:T(8,128)} %param.5) | copy-start | bytes 786436
Sparse Core Ops, SparseCore 0:
  10.2 77.5 all-gather.2
  90.7 38.2 all-reduce.3
  187.6 104.8 reduce-scatter.1
  299.3 124.7 all-reduce.5
  427.6 73.9 all-gather.4
  504.0 38.2 all-reduce.7
where the time goes:
time: 630 us; the launch traced here: 629 us
  waiting for transfers between devices  401 us (64%)
  matrix products  144 us (23%)
  local copies, waits for them, and re-layouts  64.8 us (10%)
  between operations  14.2 us (2%)
    psum x1, waiting for transfers between devices, correct(): gram_matrix = lax.psum(mult_tn(local_vectors, image), ('row', 'col'))  127 us
    reduce_scatter x1, waiting for transfers between devices, on_device(): lax.psum_scatter(mult(matrix, vec_cols), 'col', scatter_dimension=0, tile...  105 us
    all_gather x1, waiting for transfers between devices, on_device(): vec_rows = lax.all_gather(reflectors, 'col', axis=0, tiled=True)  79.8 us
    dot_general x2, matrix products, mult_nt(): lax.dot_general(left, right, (((1,), (1,)), ((), ())), precision=lax.Prec...  78.3 us
    unnamed x10, local copies, waits for them, and re-layouts  64.8 us
    dot_general x4, matrix products, mult(): jnp.dot(left, right, precision=lax.Precision.HIGHEST, preferred_element_t...  62.5 us
    psum x2, waiting for transfers between devices, broadcast(): return lax.psum(jnp.where(mine, value, jnp.zeros_like(value)), axis)  45.2 us
    all_gather x1, waiting for transfers between devices, on_device(): corr_rows = lax.all_gather(correction, 'col', axis=0, tiled=True)  42.7 us
  transfers between devices with their start and end apart: 6, of which 6 were waited for; matrix products, arithmetic and copies ran while one was open for 10% of the time, Pallas kernels for 0%

commit v1 on v0

v1 whole, which is shorter than its diff:
```python
import functools

import jax
import jax.numpy as jnp
from jax import lax
from jax.experimental import pallas as pl
from jax.experimental.pallas import tpu as pltpu
from jax.sharding import PartitionSpec as P

F32 = jnp.float32
BF16 = jnp.bfloat16
VMEM_LIMIT = 48 * 1024 * 1024


def split(value):
    high = value.astype(BF16)
    return high, (value - high.astype(F32)).astype(BF16)


def dot(left, right):
    return jnp.dot(left, right, preferred_element_type=F32)


def dot3(left, right):
    (left_high, left_low), (right_high, right_low) = left, right
    return dot(left_high, right_high) + dot(left_low, right_high) + dot(left_high, right_low)


def mult(left, right, dims=((1,), (0,))):
    return lax.dot_general(
        left, right, (dims, ((), ())), precision=lax.Precision.HIGH, preferred_element_type=F32
    )


def image_kernel(matrix_ref, vec_ref, out_ref, total):
    step = pl.program_id(0)
    product = dot3(split(vec_ref[...].T), split(matrix_ref[...]))

    @pl.when(step == 0)
    def _():
        total[...] = product

    @pl.when(step > 0)
    def _():
        total[...] += product

    @pl.when(step == pl.num_programs(0) - 1)
    def _():
        out_ref[...] = total[...].T


def image_part(matrix, vec_rows):
    (rows, cols), width = matrix.shape, vec_rows.shape[1]
    block = min(512, rows)
    return pl.pallas_call(
        image_kernel,
        grid=(rows // block,),
        out_shape=jax.ShapeDtypeStruct((cols, width), F32),
        in_specs=[
            pl.BlockSpec((block, cols), lambda i: (i, 0)),
            pl.BlockSpec((block, width), lambda i: (i, 0)),
        ],
        out_specs=pl.BlockSpec((cols, width), lambda i: (0, 0)),
        scratch_shapes=[pltpu.VMEM((width, cols), F32)],
        compiler_params=pltpu.CompilerParams(vmem_limit_bytes=VMEM_LIMIT),
        cost_estimate=pl.CostEstimate(
            flops=6 * rows * cols * width,
            bytes_accessed=4 * rows * (cols + width),
            transcendentals=0,
        ),
    )(matrix, vec_rows)


def update_kernel(matrix_ref, vec_ref, image_ref, vec_side_ref, image_side_ref, out_ref, high, low):
    width = vec_ref.shape[1]

    @pl.when(pl.program_id(0) == 0)
    def _():
        high[:width, :], low[:width, :] = split(vec_side_ref[...].T)
        high[width:, :], low[width:, :] = split(image_side_ref[...].T)

    product = dot3(split(vec_ref[...]), (high[:width, :], low[:width, :]))
    product += dot3(split(image_ref[...]), (high[width:, :], low[width:, :]))
    out_ref[...] = matrix_ref[...] - product


def update(matrix, vec_rows, image_rows, vec_side, image_side):
    (rows, cols), width = matrix.shape, vec_rows.shape[1]
    block = min(512, rows)
    row_block = lambda size: pl.BlockSpec((block, size), lambda i: (i, 0))
    whole = pl.BlockSpec((cols, width), lambda i: (0, 0))
    return pl.pallas_call(
        update_kernel,
        grid=(rows // block,),
        out_shape=jax.ShapeDtypeStruct((rows, cols), F32),
        in_specs=[row_block(cols), row_block(width), row_block(width), whole, whole],
        out_specs=row_block(cols),
        scratch_shapes=[pltpu.VMEM((2 * width, cols), BF16)] * 2,
        compiler_params=pltpu.CompilerParams(vmem_limit_bytes=VMEM_LIMIT),
        cost_estimate=pl.CostEstimate(
            flops=12 * rows * cols * width,
            bytes_accessed=8 * rows * (cols + width),
            transcendentals=0,
        ),
    )(matrix, vec_rows, image_rows, vec_side, image_side)


def shifted(value, n_rows, step):
    return lax.ppermute(value, "row", [(i, (i + step) % n_rows) for i in range(n_rows)])


def gather_row(value, n_rows):
    parts = jnp.stack([value] + [shifted(value, n_rows, step) for step in range(1, n_rows)])
    row = lax.axis_index("row")
    ordered = [
        lax.dynamic_index_in_dim(parts, (row + n_rows - i) % n_rows, 0, keepdims=False)
        for i in range(n_rows)
    ]
    return jnp.concatenate(ordered, axis=0)


def sum_row(value, n_rows):
    return sum((shifted(value, n_rows, step) for step in range(1, n_rows)), value)


def scatter_row(value, n_rows):
    row = lax.axis_index("row")
    size = value.shape[0] // n_rows
    share = lambda i: lax.dynamic_slice_in_dim(value, i % n_rows * size, size, 0)
    total = share(row)
    for step in range(1, n_rows):
        total = total + shifted(share(row + step), n_rows, step)
    return total


def gather_col(value):
    return lax.all_gather(value, "col", axis=0, tiled=True)


def on_device(n_rows, n_cols, matrix, reflectors, factor):
    devices = [(r * n_cols + c, c * n_rows + r) for r in range(n_rows) for c in range(n_cols)]
    vec_rows = gather_col(reflectors)
    vec_share = lax.ppermute(reflectors, ("row", "col"), [(b, d) for d, b in devices])
    vec_cols = gather_row(vec_share, n_rows)

    image_share = scatter_row(image_part(matrix, vec_rows), n_rows)
    image_cols = gather_row(image_share, n_rows)
    image = lax.ppermute(image_share, ("row", "col"), devices)
    image_rows = gather_col(image)

    gram = sum_row(mult(vec_rows, image_rows, ((0,), (0,))), n_rows)
    inner = mult(mult(factor, gram, ((0,), (0,))), factor)
    correction = mult(image, factor) - 0.5 * mult(reflectors, inner)
    vec_side = mult(image_cols, factor) - 0.5 * mult(vec_cols, inner + inner.T)
    image_side = mult(vec_cols, factor, ((1,), (1,)))
    updated = update(matrix, vec_rows, image_rows, vec_side, image_side)
    return updated, correction


def solution(mesh):
    return jax.shard_map(
        functools.partial(on_device, mesh.shape["row"], mesh.shape["col"]),
        mesh=mesh,
        in_specs=(P("row", "col"), P(("row", "col"), None), P()),
        out_specs=(P("row", "col"), P(("row", "col"), None)),
        check_vma=False,
    )
```

time: 630 us -> 305 us (0.48)
  waiting for transfers between devices: 401 us -> 160 us
  matrix products: 144 us -> 18.8 us
  Pallas kernels: 0 us -> 64 us
  local copies, waits for them, and re-layouts: 64.8 us -> 0.99 us
  starting transfers between devices: 0.24 us -> 45.4 us
    psum x3 -> x0, waiting for transfers between devices: 172 us -> none  [the longest x1 127 us: correct(): gram_matrix = lax.psum(mult_tn(local_vectors, image), ('row', 'col'))]
    dot_general x8, matrix products: 144 us -> 18.8 us  [mult(): lax.dot_general(left, right, (dims, ((), ())), precision=lax.Precision.HI...]
    reduce_scatter x1 -> x0, waiting for transfers between devices: 105 us -> none  [on_device(): lax.psum_scatter(mult(matrix, vec_cols), 'col', scatter_dimension=0, tile...]
    pallas_call x0 -> x2, Pallas kernels: none -> 64 us  [the longest x1 39.3 us: update(): pl.pallas_call(update_kernel, grid=(rows // block,), out_shape=jax.ShapeD...]
    unnamed x10, local copies, waits for them, and re-layouts: 64.8 us -> 0.82 us
    ppermute x0 -> x6, starting transfers between devices: none -> 45.3 us  [the longest x4 43.9 us: shifted(): lax.ppermute(value, 'row', [(i, (i + step) % n_rows) for i in range(n_row...]
    ppermute x0 -> x6, waiting for transfers between devices: none -> 29.4 us  [the longest x4 29.4 us: shifted(): lax.ppermute(value, 'row', [(i, (i + step) % n_rows) for i in range(n_row...]
    all_gather x2, waiting for transfers between devices: 123 us -> 130 us  [gather_col(): return lax.all_gather(value, 'col', axis=0, tiled=True)]
  transfers between devices with their start and end apart: 6 -> 8, of which waited for: 6 -> 5; matrix products, arithmetic and copies ran while one was open for 10% -> 5% of each run, Pallas kernels for 0% -> 0%
where the time goes in v1:
time: 305 us
  waiting for transfers between devices  160 us (52%)
  Pallas kernels  64 us (21%)
  starting transfers between devices  45.4 us (15%)
  matrix products  18.8 us (6%)
  between operations  14.2 us (5%)
    all_gather x2, waiting for transfers between devices, gather_col(): return lax.all_gather(value, 'col', axis=0, tiled=True)  130 us
    ppermute x4, starting transfers between devices, shifted(): lax.ppermute(value, 'row', [(i, (i + step) % n_rows) for i in range(n_row...  43.9 us
    pallas_call x1, Pallas kernels, update(): pl.pallas_call(update_kernel, grid=(rows // block,), out_shape=jax.ShapeD...  39.3 us
    ppermute x4, waiting for transfers between devices, shifted(): lax.ppermute(value, 'row', [(i, (i + step) % n_rows) for i in range(n_row...  29.4 us
    pallas_call x1, Pallas kernels, image_part(): pl.pallas_call(image_kernel, grid=(rows // block,), out_shape=jax.ShapeDt...  24.7 us
    dot_general x8, matrix products, mult(): lax.dot_general(left, right, (dims, ((), ())), precision=lax.Precision.HI...  18.8 us
  transfers between devices with their start and end apart: 8, of which 5 were waited for; matrix products, arithmetic and copies ran while one was open for 5% of the time, Pallas kernels for 0%

profile of v1, /device:TPU:0, one launch (start us, length us, event | category | flops | bytes accessed | tf_op | source)
XLA Modules:
  0.0 304.6 jit_solution(15321379438698190040)
XLA Ops:
  7.2 0.7 all-gather.3.cloned.1.call-update
  8.0 79.8 %all-gather.3.cloned.1.call-done.vec_ref = f32[8192,256]{1,0:T(8,128)} async-done(((f32[512,256]{1,0:T(8,128)}), f32[8192,256]{1,0:T(8,128)}) %all-gather.3.cloned.1.call-update) | async-done | bytes 8388624 | tf_op jit(solution)/shard_map/all_gather | solution.py:137
  87.8 24.7 %shard_map.50 = f32[1024,256]{1,0:T(8,128)S(1)} custom-call(f32[8192,1024]{1,0:T(8,128)} %matrix_ref.3, f32[8192,256]{1,0:T(8,128)} %all-gather.3.cloned.1.call-done.vec_ref), custom_call_target="tpu_custom_call" | custom-call | flops 12884901888 | bytes 41943040 | tf_op jit(solution)/shard_map/pallas_call | solution.py:55
  112.5 1.5 collective-permute-start
  114.1 12.6 %collective-permute-done = f32[512,256]{1,0:T(8,128)S(1)} collective-permute-done((f32[512,256]{1,0:T(8,128)S(1)}, f32[512,256]{1,0:T(8,128)S(1)}, u32[]{:S(2)}, u32[]{:S(2)}) %collective-permute-start) | collective-permute-done | bytes 524320 | tf_op jit(solution)/shard_map/ppermute | solution.py:109
  126.8 0.7 collective-permute-start.1
  127.5 0.8 copy-done.2
  128.3 0.7 collective-permute-start.3
  129.0 39.0 %collective-permute-start.4 = (f32[512,256]{1,0:T(8,128)S(1)}, f32[512,256]{1,0:T(8,128)S(1)}, u32[]{:S(2)}, u32[]{:S(2)}) collective-permute-start(f32[512,256]{1,0:T(8,128)S(1)} %collective-permute-done.3), channel_id=1, source_target_pairs={{0,16},{16,0},{1,17},{17,1},{2,18},{18,2},{3,19},{19,3},{4,20},{20... | collective-permute-start | bytes 1572872 | tf_op jit(solution)/shard_map/ppermute | solution.py:109
  168.0 12.5 %collective-permute-done.4 = f32[512,256]{1,0:T(8,128)S(1)} collective-permute-done((f32[512,256]{1,0:T(8,128)S(1)}, f32[512,256]{1,0:T(8,128)S(1)}, u32[]{:S(2)}, u32[]{:S(2)}) %collective-permute-start.4) | collective-permute-done | bytes 524320 | tf_op jit(solution)/shard_map/ppermute | solution.py:109
  180.7 0.6 fusion.6.image_side_ref
  181.3 1.8 collective-permute-start.2
  183.2 49.8 %all-gather.5.cloned.1.call-done.image_ref = f32[8192,256]{1,0:T(8,128)} async-done(((f32[512,256]{1,0:T(8,128)}), f32[8192,256]{1,0:T(8,128)}) %all-gather.5.cloned.1.call-update) | async-done | bytes 8388624 | tf_op jit(solution)/shard_map/all_gather | solution.py:137
  233.0 11.6 %convolution_bitcast_fusion = f32[256,256]{0,1:T(8,128)S(1)} fusion(f32[8192,256]{1,0:T(8,128)} %all-gather.5.cloned.1.call-done.image_ref, f32[8192,256]{1,0:T(8,128)} %all-gather.3.cloned.1.call-done.vec_ref), kind=kOutput, calls=%fused_computation.13 | convolution fusion | flops 3221225472 | bytes 17039360 | tf_op jit(solution)/shard_map/dot_general | solution.py:30
  244.6 1.5 collective-permute-start.5
  246.2 1.2 fusion.14
  247.3 1.6 fusion.2
  248.9 4.3 %collective-permute-done.5 = f32[256,256]{0,1:T(8,128)S(1)} collective-permute-done((f32[256,256]{0,1:T(8,128)S(1)}, f32[256,256]{0,1:T(8,128)S(1)}, u32[]{:S(2)}, u32[]{:S(2)}) %collective-permute-start.5) | collective-permute-done | bytes 262176 | tf_op jit(solution)/shard_map/ppermute | solution.py:109
  253.1 0.3 fusion.15
  253.4 0.4 fusion.20
  254.0 1.4 fusion.1
  255.4 1.8 fusion.vec_side_ref
  257.2 1.2 convolution_subtract_fusion
  258.4 39.3 %shard_map.51 = f32[8192,1024]{1,0:T(8,128)} custom-call(f32[8192,1024]{1,0:T(8,128)} %matrix_ref.3, f32[8192,256]{1,0:T(8,128)} %all-gather.3.cloned.1.call-done.vec_ref, f32[8192,256]{1,0:T(8,128)} %all-gather.5.cloned.1.call-done.image_ref, f32[1024,256]{1,0:T(8,128)S(1)} %fusion.vec_side_ref, f32[1024,256]{1,0:T(8,128)S(1)} %fusion.6.image_side_ref), custom_call_target="tpu_custom_call" | custom-call | flops 25769803776 | bytes 83886080 | tf_op jit(solution)/shard_map/pallas_call | solution.py:92
  (19 shorter events, 0.6 us)
Async XLA Ops:
  7.2 173.6 %copy-start = (f32[256,256]{1,0:T(8,128)S(1)}, f32[256,256]{1,0:T(8,128)}, u32[]{:S(2)}) copy-start(f32[256,256]{1,0:T(8,128)} %param.5) | copy-start | bytes 786436
  7.2 80.6 %all-gather.3.cloned.1.call-start = ((), (), s32[]{:S(2)}) async-start(), calls=%async_computation | async-start | bytes 8912896 | tf_op jit(solution)/shard_map/all_gather | solution.py:137
  7.9 225.1 %all-gather.5.cloned.1.call-start = ((), (), s32[]{:S(2)}) async-start(), calls=%async_computation.1 | async-start | bytes 8912896 | tf_op jit(solution)/shard_map/all_gather | solution.py:137
  8.0 120.3 %copy-start.4 = (f32[512,256]{1,0:T(8,128)S(1)}, f32[512,256]{1,0:T(8,128)}, u32[]{:S(2)}) copy-start(f32[512,256]{1,0:T(8,128)} %param.4) | copy-start | bytes 1572868
  112.5 14.2 %collective-permute-start = (f32[512,256]{1,0:T(8,128)S(1)}, f32[512,256]{1,0:T(8,128)S(1)}, u32[]{:S(2)}, u32[]{:S(2)}) collective-permute-start(f32[512,256]{1,0:T(8,128)S(1)} %constant_dynamic-slice_fusion), channel_id=1, source_target_pairs={{0,16},{16,0},{1,17},{17,1},{2,18},{18,2},{3,19},{19,3},{4,20},{20... | collective-permute-start | bytes 1572872 | tf_op jit(solution)/shard_map/ppermute | solution.py:109
  126.8 0.7 collective-permute-start.1
  127.5 0.8 copy-start.2
  128.3 0.7 collective-permute-start.3
  129.0 51.5 %collective-permute-start.4 = (f32[512,256]{1,0:T(8,128)S(1)}, f32[512,256]{1,0:T(8,128)S(1)}, u32[]{:S(2)}, u32[]{:S(2)}) collective-permute-start(f32[512,256]{1,0:T(8,128)S(1)} %collective-permute-done.3), channel_id=1, source_target_pairs={{0,16},{16,0},{1,17},{17,1},{2,18},{18,2},{3,19},{19,3},{4,20},{20... | collective-permute-start | bytes 1572872 | tf_op jit(solution)/shard_map/ppermute | solution.py:109
  181.3 64.8 %collective-permute-start.2 = (f32[512,256]{1,0:T(8,128)S(1)}, f32[512,256]{1,0:T(8,128)}, u32[]{:S(2)}, u32[]{:S(2)}) collective-permute-start(f32[512,256]{1,0:T(8,128)S(1)} %dynamic-slice_add_fusion), channel_id=1, source_target_pairs={{0,16},{16,0},{1,17},{17,1},{2,18},{18,2},{3,19},{19,3},{4,20},{20... | collective-permute-start | bytes 1572872 | tf_op jit(solution)/shard_map/ppermute | solution.py:109
  244.6 12.6 %copy-start.3 = (f32[512,256]{1,0:T(8,128)S(1)}, f32[512,256]{1,0:T(8,128)}, u32[]{:S(2)}) copy-start(f32[512,256]{1,0:T(8,128)} %copy-done.2) | copy-start | bytes 1572868
  244.6 8.5 %collective-permute-start.5 = (f32[256,256]{0,1:T(8,128)S(1)}, f32[256,256]{0,1:T(8,128)S(1)}, u32[]{:S(2)}, u32[]{:S(2)}) collective-permute-start(f32[256,256]{0,1:T(8,128)S(1)} %convolution_bitcast_fusion), channel_id=1, source_target_pairs={{0,16},{16,0},{1,17},{17,1},{2,18},{18,2},{3,19},{19,3},{4,20},{20... | collective-permute-start | bytes 786440 | tf_op jit(solution)/shard_map/ppermute | solution.py:109
  258.4 39.3 %copy-start.1 = (f32[256,256]{1,0:T(8,128)S(1)}, f32[256,256]{1,0:T(8,128)}, u32[]{:S(2)}) copy-start(f32[256,256]{1,0:T(8,128)} %param.5) | copy-start | bytes 786436
Sparse Core Ops, SparseCore 0:
  10.2 77.5 all-gather.2
  128.4 104.5 all-gather.4

commit v2 on v1

--- a/solution.py
+++ b/solution.py
@@ -10,6 +10,7 @@
 F32 = jnp.float32
 BF16 = jnp.bfloat16
 VMEM_LIMIT = 48 * 1024 * 1024
+GATHER_VMEM_LIMIT = 56 * 1024 * 1024
 
 
 def split(value):
@@ -17,13 +18,13 @@
     return high, (value - high.astype(F32)).astype(BF16)
 
 
-def dot(left, right):
-    return jnp.dot(left, right, preferred_element_type=F32)
-
-
 def dot3(left, right):
     (left_high, left_low), (right_high, right_low) = left, right
-    return dot(left_high, right_high) + dot(left_low, right_high) + dot(left_high, right_low)
+    return jnp.dot(
+        jnp.concatenate([left_high, left_low, left_high], axis=1),
+        jnp.concatenate([right_high, right_high, right_low], axis=0),
+        preferred_element_type=F32,
+    )
 
 
 def mult(left, right, dims=((1,), (0,))):
@@ -32,43 +33,200 @@
     )
 
 
-def image_kernel(matrix_ref, vec_ref, out_ref, total):
-    step = pl.program_id(0)
-    product = dot3(split(vec_ref[...].T), split(matrix_ref[...]))
-
-    @pl.when(step == 0)
-    def _():
-        total[...] = product
-
-    @pl.when(step > 0)
-    def _():
-        total[...] += product
-
-    @pl.when(step == pl.num_programs(0) - 1)
-    def _():
-        out_ref[...] = total[...].T
-
-
-def image_part(matrix, vec_rows):
-    (rows, cols), width = matrix.shape, vec_rows.shape[1]
-    block = min(512, rows)
-    return pl.pallas_call(
-        image_kernel,
-        grid=(rows // block,),
-        out_shape=jax.ShapeDtypeStruct((cols, width), F32),
-        in_specs=[
-            pl.BlockSpec((block, cols), lambda i: (i, 0)),
-            pl.BlockSpec((block, width), lambda i: (i, 0)),
-        ],
-        out_specs=pl.BlockSpec((cols, width), lambda i: (0, 0)),
-        scratch_shapes=[pltpu.VMEM((width, cols), F32)],
-        compiler_params=pltpu.CompilerParams(vmem_limit_bytes=VMEM_LIMIT),
+def signed(index):
+    return (index + 1) // 2 * (1 - index % 2 * 2)
+
+
+def gather_kernel(n_rows, n_cols, send_cols, left_ref, block_ref, *refs):
+    if send_cols:
+        out_ref, rows_ref, cols_ref, *refs = refs
+    else:
+        out_ref, rows_ref, *refs = refs
+    held, left, total, send_sem, recv_sem, left_sem, rows_sem, own_sem, *refs = refs
+    n_chips = n_cols // 2
+    near = 1 << (n_chips.bit_length() - 1) // 2
+    far = n_chips // near
+    row, me = lax.axis_index("row"), lax.axis_index("col")
+    my_far, my_near, my_core = me // (2 * near), me // 2 % near, me % 2
+    size = block_ref.shape[0]
+
+    def at(far_pos, near_pos, core):
+        return (far_pos * near + near_pos) * 2 + core
+
+    neighbours = [
+        (my_far + 1 < far, at(my_far + 1, my_near, my_core)),
+        (my_far > 0, at(my_far - 1, my_near, my_core)),
+        (my_near + 1 < near, at(my_far, my_near + 1, my_core)),
+        (my_near > 0, at(my_far, my_near - 1, my_core)),
+        (my_core >= 0, at(my_far, my_near, 1 - my_core)),
+    ]
+
+    def load(slot):
+        rows = pl.ds(pl.multiple_of(slot * size, size), size)
+        return pltpu.make_async_copy(left_ref.at[rows, :], left.at[slot], left_sem.at[slot])
+
+    def store(slot):
+        return pltpu.make_async_copy(held.at[slot], rows_ref.at[slot], rows_sem.at[slot])
+
+    def send(index, slot):
+        return pltpu.make_async_remote_copy(
+            src_ref=held.at[slot],
+            dst_ref=held.at[slot],
+            send_sem=send_sem.at[index, slot],
+            recv_sem=recv_sem.at[slot],
+            device_id={"col": neighbours[index][1]},
+            device_id_type=pl.DeviceIdType.MESH,
+        )
+
+    def sends(slot, far_pos, near_pos, core):
+        same = core == my_core
+        line = same & (near_pos == my_near)
+        passes = [
+            line & (far_pos <= my_far),
+            line & (far_pos >= my_far),
+            same & (near_pos <= my_near),
+            same & (near_pos >= my_near),
+            same,
+        ]
+        return [(neighbours[i][0] & passes[i], send(i, slot)) for i in range(5)]
+
+    own_copy = pltpu.make_async_copy(block_ref, held.at[me], own_sem)
+    own_copy.start()
+    load(me).start()
+
+    barrier = pltpu.get_barrier_semaphore()
+    count = 0
+    for there, device in neighbours:
+        count = count + there.astype(jnp.int32)
+
+        @pl.when(there)
+        def _(device=device):
+            pl.semaphore_signal(
+                barrier, inc=1, device_id={"col": device}, device_id_type=pl.DeviceIdType.MESH
+            )
+
+    if send_cols:
+        for step in range(1, n_rows):
+            pl.semaphore_signal(
+                barrier,
+                inc=1,
+                device_id={"row": (row + step) % n_rows},
+                device_id_type=pl.DeviceIdType.MESH,
+            )
+        count = count + (n_rows - 1)
+    pl.semaphore_wait(barrier, count)
+    own_copy.wait()
+
+    @pl.loop(0, n_cols)
+    def _(slot):
+        @pl.when(slot != me)
+        def _():
+            load(slot).start()
+
+    if send_cols:
+        cols_send_sem, cols_recv_sem, cols_own_sem = refs
+        n_cols_rows = n_rows * size
+        owner = me * n_rows // n_cols
+        offset = pl.multiple_of(me * n_rows % n_cols * size, n_cols_rows)
+        mine = left_ref.at[pl.ds(offset, n_cols_rows), :]
+        cols_own = pltpu.make_async_copy(mine, cols_ref, cols_own_sem)
+        cols_copies = [
+            pltpu.make_async_remote_copy(
+                src_ref=mine,
+                dst_ref=cols_ref,
+                send_sem=cols_send_sem.at[step - 1],
+                recv_sem=cols_recv_sem,
+                device_id={"row": (row + step) % n_rows},
+                device_id_type=pl.DeviceIdType.MESH,
+            )
+            for step in range(1, n_rows)
+        ]
+
+        @pl.when(row == owner)
+        def _():
+            cols_own.start()
+            for copy in cols_copies:
+                copy.start()
+
+    total[...] = jnp.zeros_like(total)
+    n_near = 2 * near - 1
+
+    @pl.loop(0, (far + 1) * n_near * 4)
+    def _(step):
+        distance = step // (4 * n_near) - (step // 4 % n_near > 0).astype(jnp.int32)
+        far_pos = my_far + distance * (1 - step % 2 * 2)
+        near_pos = my_near + signed(step // 4 % n_near)
+        core = (my_core + step // 2) % 2
+        valid = (distance >= 0) & (distance < far) & ((distance > 0) | (step % 2 == 0))
+        valid &= (far_pos >= 0) & (far_pos < far) & (near_pos >= 0) & (near_pos < near)
+
+        @pl.when(valid)
+        def _():
+            slot = at(far_pos, near_pos, core)
+
+            @pl.when(slot != me)
+            def _():
+                send(4, slot).wait_recv()
+
+            for passed, copy in sends(slot, far_pos, near_pos, core):
+                pl.when(passed)(copy.start)
+            store(slot).start()
+            load(slot).wait()
+            total[...] += dot3(split(held[slot].T), split(left[slot]))
+
+    out_ref[...] = total[...].T
+
+    @pl.loop(0, n_cols)
+    def _(slot):
+        for passed, copy in sends(slot, slot // (2 * near), slot // 2 % near, slot % 2):
+            pl.when(passed)(copy.wait_send)
+        store(slot).wait()
+
+    if send_cols:
+
+        @pl.when(row == owner)
+        def _():
+            cols_own.wait()
+            for copy in cols_copies:
+                copy.wait_send()
+
+        @pl.when(row != owner)
+        def _():
+            cols_copies[0].wait_recv()
+
+
+def gather_product(left, block, n_rows, n_cols, send_cols):
+    (rows, cols), (size, width) = left.shape, block.shape
+    shapes = [(cols, width), (n_cols, size, width)] + [(n_rows * size, cols)] * send_cols
+    in_hbm = pl.BlockSpec(memory_space=pl.ANY)
+    in_vmem = pl.BlockSpec(memory_space=pltpu.VMEM)
+    dma = pltpu.SemaphoreType.DMA
+    product, gathered, *rest = pl.pallas_call(
+        functools.partial(gather_kernel, n_rows, n_cols, send_cols),
+        out_shape=[jax.ShapeDtypeStruct(shape, F32) for shape in shapes],
+        in_specs=[in_hbm, in_hbm],
+        out_specs=[in_vmem, in_hbm] + [in_hbm] * send_cols,
+        scratch_shapes=[
+            pltpu.VMEM((n_cols, size, width), F32),
+            pltpu.VMEM((n_cols, size, cols), F32),
+            pltpu.VMEM((width, cols), F32),
+            dma((5, n_cols)),
+            dma((n_cols,)),
+            dma((n_cols,)),
+            dma((n_cols,)),
+            dma,
+        ]
+        + [dma((n_rows - 1,)), dma, dma] * send_cols,
+        compiler_params=pltpu.CompilerParams(
+            collective_id=int(send_cols), has_side_effects=True, vmem_limit_bytes=GATHER_VMEM_LIMIT
+        ),
         cost_estimate=pl.CostEstimate(
             flops=6 * rows * cols * width,
             bytes_accessed=4 * rows * (cols + width),
             transcendentals=0,
         ),
-    )(matrix, vec_rows)
+    )(left, block)
+    return product, gathered.reshape(rows, width), *rest
 
 
 def update_kernel(matrix_ref, vec_ref, image_ref, vec_side_ref, image_side_ref, out_ref, high, low):
@@ -133,22 +291,15 @@
     return total
 
 
-def gather_col(value):
-    return lax.all_gather(value, "col", axis=0, tiled=True)
-
-
 def on_device(n_rows, n_cols, matrix, reflectors, factor):
     devices = [(r * n_cols + c, c * n_rows + r) for r in range(n_rows) for c in range(n_cols)]
-    vec_rows = gather_col(reflectors)
-    vec_share = lax.ppermute(reflectors, ("row", "col"), [(b, d) for d, b in devices])
-    vec_cols = gather_row(vec_share, n_rows)
-
-    image_share = scatter_row(image_part(matrix, vec_rows), n_rows)
+    image_term, vec_rows = gather_product(matrix, reflectors, n_rows, n_cols, False)
+    image_share = scatter_row(image_term, n_rows)
+    image = lax.ppermute(image_share, ("row", "col"), devices)
+    gram_term, image_rows, vec_cols = gather_product(vec_rows, image, n_rows, n_cols, True)
     image_cols = gather_row(image_share, n_rows)
-    image = lax.ppermute(image_share, ("row", "col"), devices)
-    image_rows = gather_col(image)
-
-    gram = sum_row(mult(vec_rows, image_rows, ((0,), (0,))), n_rows)
+
+    gram = sum_row(gram_term, n_rows)
     inner = mult(mult(factor, gram, ((0,), (0,))), factor)
     correction = mult(image, factor) - 0.5 * mult(reflectors, inner)
     vec_side = mult(image_cols, factor) - 0.5 * mult(vec_cols, inner + inner.T)

time: 305 us -> 203 us (0.67)
  waiting for transfers between devices: 160 us -> 19.5 us
  Pallas kernels: 64 us -> 166 us
  starting transfers between devices: 45.4 us -> 5.18 us
  between operations: 14.2 us -> 0.82 us
  matrix products: 18.8 us -> 7.52 us
    all_gather x2 -> x0, waiting for transfers between devices: 130 us -> none  [gather_col(): return lax.all_gather(value, 'col', axis=0, tiled=True)]
    pallas_call x1 -> x2, Pallas kernels: 24.7 us -> 127 us  [gather_product(): pl.pallas_call(functools.partial(gather_kernel, n_rows, n_cols, send_cols...]
    ppermute x4 -> x3, starting transfers between devices: 43.9 us -> 4.48 us  [shifted(): lax.ppermute(value, 'row', [(i, (i + step) % n_rows) for i in range(n_row...]
    dot_general x8 -> x7, matrix products: 18.8 us -> 7.52 us  [mult(): lax.dot_general(left, right, (dims, ((), ())), precision=lax.Precision.HI...]
    ppermute x4 -> x3, waiting for transfers between devices: 29.4 us -> 19.5 us  [shifted(): lax.ppermute(value, 'row', [(i, (i + step) % n_rows) for i in range(n_row...]
  transfers between devices with their start and end apart: 8 -> 4, of which waited for: 5 -> 2; matrix products, arithmetic and copies ran while one was open for 5% -> 1% of each run, Pallas kernels for 0% -> 34%
where the time goes in v2:
time: 203 us; the launch traced here: 202 us
  Pallas kernels  166 us (82%)
  waiting for transfers between devices  19.5 us (10%)
  matrix products  7.52 us (4%)
  starting transfers between devices  5.18 us (3%)
    pallas_call x2, Pallas kernels, gather_product(): pl.pallas_call(functools.partial(gather_kernel, n_rows, n_cols, send_cols...  127 us
    pallas_call x1, Pallas kernels, update(): pl.pallas_call(update_kernel, grid=(rows // block,), out_shape=jax.ShapeD...  39.3 us
    ppermute x3, waiting for transfers between devices, shifted(): lax.ppermute(value, 'row', [(i, (i + step) % n_rows) for i in range(n_row...  19.5 us
    dot_general x7, matrix products, mult(): lax.dot_general(left, right, (dims, ((), ())), precision=lax.Precision.HI...  7.52 us
    ppermute x3, starting transfers between devices, shifted(): lax.ppermute(value, 'row', [(i, (i + step) % n_rows) for i in range(n_row...  4.48 us
  transfers between devices with their start and end apart: 4, of which 2 were waited for; matrix products, arithmetic and copies ran while one was open for 1% of the time, Pallas kernels for 34%

profile of v2, /device:TPU:0, one launch (start us, length us, event | category | flops | bytes accessed | tf_op | source)
XLA Modules:
  0.0 202.3 jit_solution(11416626934571184871)
XLA Ops:
  0.6 0.0 copy-start
  0.7 58.3 %shard_map.50 = (f32[1024,256]{1,0:T(8,128)}, f32[16,512,256]{2,1,0:T(8,128)}) custom-call(f32[8192,1024]{1,0:T(8,128)} %matrix_ref.1, f32[512,256]{1,0:T(8,128)} %block_ref.1), custom_call_target="tpu_custom_call" | custom-call | flops 12884901888 | bytes 41943040 | tf_op jit(solution)/shard_map/pallas_call | solution.py:204
  59.0 1.1 constant_dynamic-slice_fusion
  60.1 1.6 collective-permute-start
  61.7 13.1 %collective-permute-done = f32[512,256]{1,0:T(8,128)S(1)} collective-permute-done((f32[512,256]{1,0:T(8,128)S(1)}, f32[512,256]{1,0:T(8,128)S(1)}, u32[]{:S(2)}, u32[]{:S(2)}) %collective-permute-start) | collective-permute-done | bytes 524320 | tf_op jit(solution)/shard_map/ppermute | solution.py:267
  74.7 1.1 dynamic-slice_add_fusion
  75.8 0.7 collective-permute-start.1
  76.6 2.8 %collective-permute-start.2 = (f32[512,256]{1,0:T(8,128)S(1)}, f32[512,256]{1,0:T(8,128)S(1)}, u32[]{:S(2)}, u32[]{:S(2)}) collective-permute-start(f32[512,256]{1,0:T(8,128)S(1)} %dynamic-slice_add_fusion), channel_id=1, source_target_pairs={{0,16},{16,0},{1,17},{17,1},{2,18},{18,2},{3,19},{19,3},{4,20},{20... | collective-permute-start | bytes 1572872 | tf_op jit(solution)/shard_map/ppermute | solution.py:267
  79.4 0.0 collective-permute-done.1.block_ref
  79.4 0.8 copy-done.1
  80.2 68.3 %shard_map.51 = (f32[256,256]{1,0:T(8,128)}, f32[16,512,256]{2,1,0:T(8,128)}, f32[1024,256]{1,0:T(8,128)}) custom-call(f32[8192,256]{1,0:T(8,128)} %bitcast.26, f32[512,256]{1,0:T(8,128)} %copy-done.1), custom_call_target="tpu_custom_call" | custom-call | flops 3221225472 | bytes 16777216 | tf_op jit(solution)/shard_map/pallas_call | solution.py:204
  148.4 0.1 collective-permute-start.3
  148.5 1.8 fusion.14.image_side_ref
  150.4 0.2 fusion.9
  150.6 0.6 fusion.2
  151.2 6.4 %collective-permute-done.3 = f32[256,256]{1,0:T(8,128)S(1)} collective-permute-done((f32[256,256]{1,0:T(8,128)}, f32[256,256]{1,0:T(8,128)S(1)}, u32[]{:S(2)}, u32[]{:S(2)}) %collective-permute-start.3) | collective-permute-done | bytes 262176 | tf_op jit(solution)/shard_map/ppermute | solution.py:267
  157.6 1.3 fusion.10
  159.0 0.4 fusion.13
  159.4 0.1 copy.5
  159.5 0.4 fusion.1
  159.9 1.8 fusion.vec_side_ref
  161.7 0.0 copy-start.2
  161.8 39.3 %shard_map.52 = f32[8192,1024]{1,0:T(8,128)} custom-call(f32[8192,1024]{1,0:T(8,128)} %matrix_ref.1, f32[8192,256]{1,0:T(8,128)} %bitcast.27, f32[8192,256]{1,0:T(8,128)} %bitcast.28, f32[1024,256]{1,0:T(8,128)S(1)} %fusion.vec_side_ref, f32[1024,256]{1,0:T(8,128)S(1)} %fusion.14.image_side_ref), custom_call_target="tpu_custom_call" | custom-call | flops 25769803776 | bytes 83886080 | tf_op jit(solution)/shard_map/pallas_call | solution.py:250
  201.1 1.2 convolution_subtract_fusion
  (6 shorter events, 0.0 us)
Async XLA Ops:
  0.6 147.9 %copy-start = (f32[256,256]{1,0:T(8,128)S(1)}, f32[256,256]{1,0:T(8,128)}, u32[]{:S(2)}) copy-start(f32[256,256]{1,0:T(8,128)} %param.5) | copy-start | bytes 786436
  0.7 158.9 %copy-start.3 = (f32[512,256]{1,0:T(8,128)S(1)}, f32[512,256]{1,0:T(8,128)}, u32[]{:S(2)}) copy-start(f32[512,256]{1,0:T(8,128)} %block_ref.1) | copy-start | bytes 1572868
  60.1 14.7 %collective-permute-start = (f32[512,256]{1,0:T(8,128)S(1)}, f32[512,256]{1,0:T(8,128)S(1)}, u32[]{:S(2)}, u32[]{:S(2)}) collective-permute-start(f32[512,256]{1,0:T(8,128)S(1)} %constant_dynamic-slice_fusion), channel_id=1, source_target_pairs={{0,16},{16,0},{1,17},{17,1},{2,18},{18,2},{3,19},{19,3},{4,20},{20... | collective-permute-start | bytes 1572872 | tf_op jit(solution)/shard_map/ppermute | solution.py:267
  75.8 3.5 %collective-permute-start.1 = (f32[512,256]{1,0:T(8,128)S(1)}, f32[512,256]{1,0:T(8,128)S(1)}, u32[]{:S(2)}, u32[]{:S(2)}) collective-permute-start(f32[512,256]{1,0:T(8,128)S(1)} %dynamic-slice_add_fusion), channel_id=1, source_target_pairs={{0,0},{1,2},{2,4},{3,6},{4,8},{5,10},{6,12},{7,14},{8,16},{9,18},{... | collective-permute-start | bytes 1572872 | tf_op jit(solution)/shard_map/ppermute | solution.py:298
  76.6 73.8 %collective-permute-start.2 = (f32[512,256]{1,0:T(8,128)S(1)}, f32[512,256]{1,0:T(8,128)S(1)}, u32[]{:S(2)}, u32[]{:S(2)}) collective-permute-start(f32[512,256]{1,0:T(8,128)S(1)} %dynamic-slice_add_fusion), channel_id=1, source_target_pairs={{0,16},{16,0},{1,17},{17,1},{2,18},{18,2},{3,19},{19,3},{4,20},{20... | collective-permute-start | bytes 1572872 | tf_op jit(solution)/shard_map/ppermute | solution.py:267
  79.4 0.8 copy-start.1
  148.4 9.2 %collective-permute-start.3 = (f32[256,256]{1,0:T(8,128)}, f32[256,256]{1,0:T(8,128)S(1)}, u32[]{:S(2)}, u32[]{:S(2)}) collective-permute-start(f32[256,256]{1,0:T(8,128)} %get-tuple-element.11), channel_id=1, source_target_pairs={{0,16},{16,0},{1,17},{17,1},{2,18},{18,2},{3,19},{19,3},{4,20},{20... | collective-permute-start | bytes 786440 | tf_op jit(solution)/shard_map/ppermute | solution.py:267
  161.7 39.3 %copy-start.2 = (f32[512,256]{1,0:T(8,128)S(1)}, f32[512,256]{1,0:T(8,128)}, u32[]{:S(2)}) copy-start(f32[512,256]{1,0:T(8,128)} %copy-done.1) | copy-start | bytes 1572868

commit v3 on v2

--- a/solution.py
+++ b/solution.py
@@ -39,7 +39,7 @@
 
 def gather_kernel(n_rows, n_cols, send_cols, left_ref, block_ref, *refs):
     if send_cols:
-        out_ref, rows_ref, cols_ref, *refs = refs
+        out_ref, rows_ref, cols_ref, sum_ref, *refs = refs
     else:
         out_ref, rows_ref, *refs = refs
     held, left, total, send_sem, recv_sem, left_sem, rows_sem, own_sem, *refs = refs
@@ -48,7 +48,7 @@
     far = n_chips // near
     row, me = lax.axis_index("row"), lax.axis_index("col")
     my_far, my_near, my_core = me // (2 * near), me // 2 % near, me % 2
-    size = block_ref.shape[0]
+    size = held.shape[1]
 
     def at(far_pos, near_pos, core):
         return (far_pos * near + near_pos) * 2 + core
@@ -90,8 +90,9 @@
         ]
         return [(neighbours[i][0] & passes[i], send(i, slot)) for i in range(5)]
 
-    own_copy = pltpu.make_async_copy(block_ref, held.at[me], own_sem)
-    own_copy.start()
+    if not send_cols:
+        own_copy = pltpu.make_async_copy(block_ref, held.at[me], own_sem)
+        own_copy.start()
     load(me).start()
 
     barrier = pltpu.get_barrier_semaphore()
@@ -113,9 +114,79 @@
                 device_id={"row": (row + step) % n_rows},
                 device_id_type=pl.DeviceIdType.MESH,
             )
-        count = count + (n_rows - 1)
+        flat = row * n_cols + me
+        source_col = flat // n_rows
+        for source_row in range(n_rows):
+
+            @pl.when(source_row * n_cols + source_col != flat)
+            def _(source_row=source_row):
+                pl.semaphore_signal(
+                    barrier,
+                    inc=1,
+                    device_id={"row": source_row, "col": source_col},
+                    device_id_type=pl.DeviceIdType.MESH,
+                )
+
+        count = count + (2 * n_rows - 1) - (source_col == me).astype(jnp.int32)
     pl.semaphore_wait(barrier, count)
-    own_copy.wait()
+    if send_cols:
+        cols_send_sem, cols_recv_sem, cols_own_sem, *refs = refs
+        shares, peers, grams, gram_own, *refs = refs
+        share_send, share_recv, peer_send, peer_recv, gram_send, gram_recv = refs
+        targets = [me * n_rows + i for i in range(n_rows)]
+
+        def share_copy(i):
+            return pltpu.make_async_remote_copy(
+                src_ref=block_ref.at[pl.ds(i * size, size), :],
+                dst_ref=shares.at[row],
+                send_sem=share_send.at[i],
+                recv_sem=share_recv.at[row],
+                device_id={"row": targets[i] // n_cols, "col": targets[i] % n_cols},
+                device_id_type=pl.DeviceIdType.MESH,
+            )
+
+        def share_own(i):
+            return pltpu.make_async_copy(
+                block_ref.at[pl.ds(i * size, size), :], shares.at[row], own_sem
+            )
+
+        for i in range(n_rows):
+            pl.when(targets[i] != flat)(share_copy(i).start)
+            pl.when(targets[i] == flat)(share_own(i).start)
+        for i in range(n_rows):
+            pl.when(targets[i] == flat)(share_own(i).wait)
+
+            @pl.when(i * n_cols + source_col != flat)
+            def _(i=i):
+                pltpu.make_async_remote_copy(
+                    src_ref=shares.at[i],
+                    dst_ref=shares.at[i],
+                    send_sem=share_send.at[i],
+                    recv_sem=share_recv.at[i],
+                    device_id={"row": targets[i] // n_cols, "col": targets[i] % n_cols},
+                    device_id_type=pl.DeviceIdType.MESH,
+                ).wait_recv()
+
+        held[me] = sum((shares[i] for i in range(1, n_rows)), shares[0])
+
+        def to_row(source, target, send_sems, recv_sems, step):
+            return pltpu.make_async_remote_copy(
+                src_ref=source,
+                dst_ref=target.at[step - 1],
+                send_sem=send_sems.at[step - 1],
+                recv_sem=recv_sems.at[step - 1],
+                device_id={"row": (row + step) % n_rows},
+                device_id_type=pl.DeviceIdType.MESH,
+            )
+
+        peer_copies = [
+            to_row(block_ref, peers, peer_send, peer_recv, step) for step in range(1, n_rows)
+        ]
+        gram_copies = [
+            to_row(gram_own, grams, gram_send, gram_recv, step) for step in range(1, n_rows)
+        ]
+    else:
+        own_copy.wait()
 
     @pl.loop(0, n_cols)
     def _(slot):
@@ -124,7 +195,6 @@
             load(slot).start()
 
     if send_cols:
-        cols_send_sem, cols_recv_sem, cols_own_sem = refs
         n_cols_rows = n_rows * size
         owner = me * n_rows // n_cols
         offset = pl.multiple_of(me * n_rows % n_cols * size, n_cols_rows)
@@ -148,6 +218,9 @@
             for copy in cols_copies:
                 copy.start()
 
+        for copy in peer_copies:
+            copy.start()
+
     total[...] = jnp.zeros_like(total)
     n_near = 2 * near - 1
 
@@ -174,7 +247,12 @@
             load(slot).wait()
             total[...] += dot3(split(held[slot].T), split(left[slot]))
 
-    out_ref[...] = total[...].T
+    if send_cols:
+        gram_own[...] = total[...].T
+        for copy in gram_copies:
+            copy.start()
+    else:
+        out_ref[...] = total[...].T
 
     @pl.loop(0, n_cols)
     def _(slot):
@@ -194,18 +272,27 @@
         def _():
             cols_copies[0].wait_recv()
 
+        for i in range(n_rows):
+            pl.when(targets[i] != flat)(share_copy(i).wait_send)
+        for copy in peer_copies + gram_copies:
+            copy.wait()
+        sum_ref[...] = sum((peers[i] for i in range(n_rows - 1)), block_ref[...])
+        out_ref[...] = sum((grams[i] for i in range(n_rows - 1)), gram_own[...])
+
 
 def gather_product(left, block, n_rows, n_cols, send_cols):
-    (rows, cols), (size, width) = left.shape, block.shape
-    shapes = [(cols, width), (n_cols, size, width)] + [(n_rows * size, cols)] * send_cols
+    (rows, cols), width = left.shape, block.shape[1]
+    size = rows // n_cols
+    shapes = [(cols, width), (n_cols, size, width)]
+    shapes += [(n_rows * size, cols), (n_rows * size, width)] * send_cols
     in_hbm = pl.BlockSpec(memory_space=pl.ANY)
     in_vmem = pl.BlockSpec(memory_space=pltpu.VMEM)
     dma = pltpu.SemaphoreType.DMA
     product, gathered, *rest = pl.pallas_call(
         functools.partial(gather_kernel, n_rows, n_cols, send_cols),
         out_shape=[jax.ShapeDtypeStruct(shape, F32) for shape in shapes],
-        in_specs=[in_hbm, in_hbm],
-        out_specs=[in_vmem, in_hbm] + [in_hbm] * send_cols,
+        in_specs=[in_hbm, in_vmem if send_cols else in_hbm],
+        out_specs=[in_vmem, in_hbm] + [in_hbm, in_vmem] * send_cols,
         scratch_shapes=[
             pltpu.VMEM((n_cols, size, width), F32),
             pltpu.VMEM((n_cols, size, cols), F32),
@@ -216,7 +303,19 @@
             dma((n_cols,)),
             dma,
         ]
-        + [dma((n_rows - 1,)), dma, dma] * send_cols,
+        + [
+            dma((n_rows - 1,)),
+            dma,
+            dma,
+            pltpu.VMEM((n_rows, size, width), F32),
+            pltpu.VMEM((n_rows - 1, n_rows * size, width), F32),
+            pltpu.VMEM((n_rows - 1, cols, width), F32),
+            pltpu.VMEM((cols, width), F32),
+            dma((n_rows,)),
+            dma((n_rows,)),
+        ]
+        * send_cols
+        + [dma((n_rows - 1,))] * (4 * send_cols),
         compiler_params=pltpu.CompilerParams(
             collective_id=int(send_cols), has_side_effects=True, vmem_limit_bytes=GATHER_VMEM_LIMIT
         ),
@@ -229,16 +328,22 @@
     return product, gathered.reshape(rows, width), *rest
 
 
-def update_kernel(matrix_ref, vec_ref, image_ref, vec_side_ref, image_side_ref, out_ref, high, low):
+def update_kernel(matrix_ref, vec_ref, image_ref, vec_side_ref, image_side_ref, out_ref, sides):
     width = vec_ref.shape[1]
 
     @pl.when(pl.program_id(0) == 0)
     def _():
-        high[:width, :], low[:width, :] = split(vec_side_ref[...].T)
-        high[width:, :], low[width:, :] = split(image_side_ref[...].T)
-
-    product = dot3(split(vec_ref[...]), (high[:width, :], low[:width, :]))
-    product += dot3(split(image_ref[...]), (high[width:, :], low[width:, :]))
+        for i, side_ref in enumerate((vec_side_ref, image_side_ref)):
+            high, low = split(side_ref[...].T)
+            for j, part in enumerate((high, high, low)):
+                sides[pl.ds((3 * i + j) * width, width), :] = part
+
+    vec_high, vec_low = split(vec_ref[...])
+    image_high, image_low = split(image_ref[...])
+    parts = [vec_high, vec_low, vec_high, image_high, image_low, image_high]
+    product = jnp.dot(
+        jnp.concatenate(parts, axis=1), sides[...], preferred_element_type=F32
+    )
     out_ref[...] = matrix_ref[...] - product
 
 
@@ -253,7 +358,7 @@
         out_shape=jax.ShapeDtypeStruct((rows, cols), F32),
         in_specs=[row_block(cols), row_block(width), row_block(width), whole, whole],
         out_specs=row_block(cols),
-        scratch_shapes=[pltpu.VMEM((2 * width, cols), BF16)] * 2,
+        scratch_shapes=[pltpu.VMEM((6 * width, cols), BF16)],
         compiler_params=pltpu.CompilerParams(vmem_limit_bytes=VMEM_LIMIT),
         cost_estimate=pl.CostEstimate(
             flops=12 * rows * cols * width,
@@ -263,43 +368,13 @@
     )(matrix, vec_rows, image_rows, vec_side, image_side)
 
 
-def shifted(value, n_rows, step):
-    return lax.ppermute(value, "row", [(i, (i + step) % n_rows) for i in range(n_rows)])
-
-
-def gather_row(value, n_rows):
-    parts = jnp.stack([value] + [shifted(value, n_rows, step) for step in range(1, n_rows)])
-    row = lax.axis_index("row")
-    ordered = [
-        lax.dynamic_index_in_dim(parts, (row + n_rows - i) % n_rows, 0, keepdims=False)
-        for i in range(n_rows)
-    ]
-    return jnp.concatenate(ordered, axis=0)
-
-
-def sum_row(value, n_rows):
-    return sum((shifted(value, n_rows, step) for step in range(1, n_rows)), value)
-
-
-def scatter_row(value, n_rows):
-    row = lax.axis_index("row")
-    size = value.shape[0] // n_rows
-    share = lambda i: lax.dynamic_slice_in_dim(value, i % n_rows * size, size, 0)
-    total = share(row)
-    for step in range(1, n_rows):
-        total = total + shifted(share(row + step), n_rows, step)
-    return total
-
-
 def on_device(n_rows, n_cols, matrix, reflectors, factor):
-    devices = [(r * n_cols + c, c * n_rows + r) for r in range(n_rows) for c in range(n_cols)]
     image_term, vec_rows = gather_product(matrix, reflectors, n_rows, n_cols, False)
-    image_share = scatter_row(image_term, n_rows)
-    image = lax.ppermute(image_share, ("row", "col"), devices)
-    gram_term, image_rows, vec_cols = gather_product(vec_rows, image, n_rows, n_cols, True)
-    image_cols = gather_row(image_share, n_rows)
-
-    gram = sum_row(gram_term, n_rows)
+    gram, image_rows, vec_cols, image_cols = gather_product(
+        vec_rows, image_term, n_rows, n_cols, True
+    )
+    size = reflectors.shape[0]
+    image = lax.dynamic_slice_in_dim(image_rows, lax.axis_index("col") * size, size, 0)
     inner = mult(mult(factor, gram, ((0,), (0,))), factor)
     correction = mult(image, factor) - 0.5 * mult(reflectors, inner)
     vec_side = mult(image_cols, factor) - 0.5 * mult(vec_cols, inner + inner.T)

time: 203 us -> 192 us (0.946)
  waiting for transfers between devices: 19.5 us -> 0 us
  Pallas kernels: 166 us -> 182 us
  starting transfers between devices: 5.18 us -> 0 us
    ppermute x4 -> x0, waiting for transfers between devices: 19.5 us -> none  [the longest x3 19.5 us: shifted(): lax.ppermute(value, 'row', [(i, (i + step) % n_rows) for i in range(n_row...]
    pallas_call x2, Pallas kernels: 127 us -> 142 us  [gather_product(): pl.pallas_call(functools.partial(gather_kernel, n_rows, n_cols, send_cols...]
    ppermute x4 -> x0, starting transfers between devices: 5.18 us -> none  [the longest x3 4.48 us: shifted(): lax.ppermute(value, 'row', [(i, (i + step) % n_rows) for i in range(n_row...]
  transfers between devices with their start and end apart: 4 -> 0, of which waited for: 2 -> 0; matrix products, arithmetic and copies ran while one was open for 1% -> 0% of each run, Pallas kernels for 34% -> 0%
where the time goes in v3:
time: 192 us; the launch traced here: 191 us
  Pallas kernels  182 us (95%)
  matrix products  8.66 us (5%)
    pallas_call x2, Pallas kernels, gather_product(): pl.pallas_call(functools.partial(gather_kernel, n_rows, n_cols, send_cols...  142 us
    pallas_call x1, Pallas kernels, update(): pl.pallas_call(update_kernel, grid=(rows // block,), out_shape=jax.ShapeD...  39.4 us
    dot_general x7, matrix products, mult(): lax.dot_general(left, right, (dims, ((), ())), precision=lax.Precision.HI...  8.66 us

profile of v3, /device:TPU:0, one launch (start us, length us, event | category | flops | bytes accessed | tf_op | source)
XLA Modules:
  0.0 191.4 jit_solution(7106702729371376680)
XLA Ops:
  0.6 0.0 copy-start
  0.6 58.2 %shard_map.50 = (f32[1024,256]{1,0:T(8,128)}, f32[16,512,256]{2,1,0:T(8,128)}) custom-call(f32[8192,1024]{1,0:T(8,128)} %matrix_ref.1, f32[512,256]{1,0:T(8,128)} %block_ref.1), custom_call_target="tpu_custom_call" | custom-call | flops 12884901888 | bytes 41943040 | tf_op jit(solution)/shard_map/pallas_call | solution.py:291
  58.8 84.3 %shard_map.51 = (f32[256,256]{1,0:T(8,128)}, f32[16,512,256]{2,1,0:T(8,128)}, f32[1024,256]{1,0:T(8,128)}, f32[1024,256]{1,0:T(8,128)}) custom-call(f32[8192,256]{1,0:T(8,128)} %bitcast.23, f32[1024,256]{1,0:T(8,128)} %get-tuple-element.9.block_ref), custom_call_target="tpu_custom_call" | custom-call | flops 3221225472 | bytes 16777216 | tf_op jit(solution)/shard_map/pallas_call | solution.py:291
  143.1 0.0 copy-start.1
  143.1 0.0 copy-done
  143.1 1.4 fusion.7
  144.6 0.4 fusion.8
  145.0 0.1 copy.5
  145.1 1.8 fusion.6
  146.9 1.8 fusion.vec_side_ref
  148.7 0.0 copy-done.1
  148.7 0.6 fusion.9.image_side_ref
  149.4 0.0 copy-start.2
  149.4 39.4 %shard_map.52 = f32[8192,1024]{1,0:T(8,128)} custom-call(f32[8192,1024]{1,0:T(8,128)} %matrix_ref.1, f32[8192,256]{1,0:T(8,128)} %bitcast.24, f32[8192,256]{1,0:T(8,128)} %bitcast.21, f32[1024,256]{1,0:T(8,128)S(1)} %fusion.vec_side_ref, f32[1024,256]{1,0:T(8,128)S(1)} %fusion.9.image_side_ref), custom_call_target="tpu_custom_call" | custom-call | flops 25769803776 | bytes 83886080 | tf_op jit(solution)/shard_map/pallas_call | solution.py:355
  188.8 1.4 fusion.3
  190.2 0.0 copy-done.2
  190.2 1.2 fusion.2
Async XLA Ops:
  0.6 142.5 %copy-start = (f32[256,256]{1,0:T(8,128)S(1)}, f32[256,256]{1,0:T(8,128)}, u32[]{:S(2)}) copy-start(f32[256,256]{1,0:T(8,128)} %param.5) | copy-start | bytes 786436
  143.1 5.6 %copy-start.1 = (f32[1024,256]{1,0:T(8,128)S(1)}, f32[1024,256]{1,0:T(8,128)}, u32[]{:S(2)}) copy-start(f32[1024,256]{1,0:T(8,128)} %get-tuple-element.12) | copy-start | bytes 3145732
  149.4 40.8 %copy-start.2 = (f32[512,256]{1,0:T(8,128)S(1)}, f32[512,256]{1,0:T(8,128)}, u32[]{:S(2)}) copy-start(f32[512,256]{1,0:T(8,128)} %block_ref.1) | copy-start | bytes 1572868

commit v4 on v3

--- a/solution.py
+++ b/solution.py
@@ -9,8 +9,8 @@
 
 F32 = jnp.float32
 BF16 = jnp.bfloat16
-VMEM_LIMIT = 48 * 1024 * 1024
-GATHER_VMEM_LIMIT = 56 * 1024 * 1024
+MIB = 1024 * 1024
+LINK_WEIGHT = 16
 
 
 def split(value):
@@ -291,7 +291,10 @@
     product, gathered, *rest = pl.pallas_call(
         functools.partial(gather_kernel, n_rows, n_cols, send_cols),
         out_shape=[jax.ShapeDtypeStruct(shape, F32) for shape in shapes],
-        in_specs=[in_hbm, in_vmem if send_cols else in_hbm],
+        in_specs=[
+            pl.BlockSpec(memory_space=pltpu.HBM),
+            in_vmem if send_cols else in_hbm,
+        ],
         out_specs=[in_vmem, in_hbm] + [in_hbm, in_vmem] * send_cols,
         scratch_shapes=[
             pltpu.VMEM((n_cols, size, width), F32),
@@ -317,11 +320,11 @@
         * send_cols
         + [dma((n_rows - 1,))] * (4 * send_cols),
         compiler_params=pltpu.CompilerParams(
-            collective_id=int(send_cols), has_side_effects=True, vmem_limit_bytes=GATHER_VMEM_LIMIT
+            collective_id=int(send_cols), has_side_effects=True, vmem_limit_bytes=(42 if send_cols else 56) * MIB
         ),
         cost_estimate=pl.CostEstimate(
             flops=6 * rows * cols * width,
-            bytes_accessed=4 * rows * (cols + width),
+            bytes_accessed=4 * rows * (cols + LINK_WEIGHT * width),
             transcendentals=0,
         ),
     )(left, block)
@@ -349,7 +352,7 @@
 
 def update(matrix, vec_rows, image_rows, vec_side, image_side):
     (rows, cols), width = matrix.shape, vec_rows.shape[1]
-    block = min(512, rows)
+    block = min(256, rows)
     row_block = lambda size: pl.BlockSpec((block, size), lambda i: (i, 0))
     whole = pl.BlockSpec((cols, width), lambda i: (0, 0))
     return pl.pallas_call(
@@ -359,7 +362,7 @@
         in_specs=[row_block(cols), row_block(width), row_block(width), whole, whole],
         out_specs=row_block(cols),
         scratch_shapes=[pltpu.VMEM((6 * width, cols), BF16)],
-        compiler_params=pltpu.CompilerParams(vmem_limit_bytes=VMEM_LIMIT),
+        compiler_params=pltpu.CompilerParams(vmem_limit_bytes=20 * MIB),
         cost_estimate=pl.CostEstimate(
             flops=12 * rows * cols * width,
             bytes_accessed=8 * rows * (cols + width),

time: 192 us -> 203 us (1.057)
  local copies, waits for them, and re-layouts: 0.15 us -> 9.53 us
  Pallas kernels: 182 us -> 186 us
  matrix products: 8.66 us -> 5.16 us
    unnamed x6 -> x12, local copies, waits for them, and re-layouts: 0.02 us -> 9.4 us
    pallas_call x1, Pallas kernels: 39.4 us -> 45.2 us  [update(): pl.pallas_call(update_kernel, grid=(rows // block,), out_shape=jax.ShapeD...]
    dot_general x7, matrix products: 8.66 us -> 5.16 us  [mult(): lax.dot_general(left, right, (dims, ((), ())), precision=lax.Precision.HI...]
    pallas_call x2, Pallas kernels: 142 us -> 140 us  [gather_product(): pl.pallas_call(functools.partial(gather_kernel, n_rows, n_cols, send_cols...]
where the time goes in v4:
time: 203 us; the launch traced here: 201 us
  Pallas kernels  186 us (92%)
  local copies, waits for them, and re-layouts  9.53 us (5%)
  matrix products  5.16 us (3%)
    pallas_call x2, Pallas kernels, gather_product(): pl.pallas_call(functools.partial(gather_kernel, n_rows, n_cols, send_cols...  140 us
    pallas_call x1, Pallas kernels, update(): pl.pallas_call(update_kernel, grid=(rows // block,), out_shape=jax.ShapeD...  45.2 us
    unnamed x12, local copies, waits for them, and re-layouts  9.4 us
    dot_general x7, matrix products, mult(): lax.dot_general(left, right, (dims, ((), ())), precision=lax.Precision.HI...  5.16 us

profile of v4, /device:TPU:0, one launch (start us, length us, event | category | flops | bytes accessed | tf_op | source)
XLA Modules:
  0.0 201.0 jit_solution(4997370176898087895)
XLA Ops:
  0.6 0.0 copy-start
  0.6 58.3 %shard_map.50 = (f32[1024,256]{1,0:T(8,128)}, f32[16,512,256]{2,1,0:T(8,128)}) custom-call(f32[8192,1024]{1,0:T(8,128)} %matrix_ref.1, f32[512,256]{1,0:T(8,128)} %block_ref.1), custom_call_target="tpu_custom_call" | custom-call | flops 12884901888 | bytes 167772160 | tf_op jit(solution)/shard_map/pallas_call | solution.py:291
  58.9 0.0 copy-start.4
  58.9 1.2 copy-done.4
  60.1 82.1 %shard_map.51 = (f32[256,256]{1,0:T(8,128)S(1)}, f32[16,512,256]{2,1,0:T(8,128)S(1)}, f32[1024,256]{1,0:T(8,128)S(1)}, f32[1024,256]{1,0:T(8,128)S(1)}) custom-call(f32[8192,256]{1,0:T(8,128)} %bitcast.23, f32[1024,256]{1,0:T(8,128)S(1)} %copy-done.4), custom_call_target="tpu_custom_call" | custom-call | flops 3221225472 | bytes 142606336 | tf_op jit(solution)/shard_map/pallas_call | solution.py:291
  142.2 0.0 copy-start.1
  142.2 3.2 %copy-done.1 = f32[16,512,256]{2,1,0:T(8,128)} copy-done((f32[16,512,256]{2,1,0:T(8,128)}, f32[16,512,256]{2,1,0:T(8,128)S(1)}, u32[]{:S(2)}) %copy-start.1) | copy-done | bytes 8388632
  145.4 0.0 copy-done
  145.4 0.4 fusion.7
  145.8 0.4 fusion.8
  146.2 0.1 copy.5
  146.4 0.0 copy-start.2
  146.4 0.6 fusion.6
  147.0 0.6 fusion.vec_side_ref
  147.5 0.6 fusion.9.image_side_ref
  148.2 1.6 copy-done.2
  149.7 0.0 copy-start.3
  149.7 3.4 %copy-done.3 = f32[16,512,256]{2,1,0:T(8,128)S(1)} copy-done((f32[16,512,256]{2,1,0:T(8,128)S(1)}, f32[16,512,256]{2,1,0:T(8,128)}, u32[]{:S(2)}) %copy-start.3) | copy-done | bytes 8388632
  153.1 0.0 copy-start.5
  153.1 45.2 %shard_map.52 = f32[8192,1024]{1,0:T(8,128)} custom-call(f32[8192,1024]{1,0:T(8,128)} %matrix_ref.1, f32[8192,256]{1,0:T(8,128)S(1)} %bitcast.24, f32[8192,256]{1,0:T(8,128)S(1)} %bitcast.22, f32[1024,256]{1,0:T(8,128)S(1)} %fusion.vec_side_ref, f32[1024,256]{1,0:T(8,128)S(1)} %fusion.9.image_side_ref), custom_call_target="tpu_custom_call" | custom-call | flops 25769803776 | bytes 83886080 | tf_op jit(solution)/shard_map/pallas_call | solution.py:358
  198.3 1.4 fusion.3
  199.8 0.0 copy-done.5
  199.8 1.2 fusion.2
Async XLA Ops:
  0.6 144.8 %copy-start = (f32[256,256]{1,0:T(8,128)S(1)}, f32[256,256]{1,0:T(8,128)}, u32[]{:S(2)}) copy-start(f32[256,256]{1,0:T(8,128)} %param.5) | copy-start | bytes 786436
  58.9 1.2 copy-start.4
  142.2 3.2 %copy-start.1 = (f32[16,512,256]{2,1,0:T(8,128)}, f32[16,512,256]{2,1,0:T(8,128)S(1)}, u32[]{:S(2)}) copy-start(f32[16,512,256]{2,1,0:T(8,128)S(1)} %get-tuple-element.10) | copy-start | bytes 25165828
  146.4 3.4 %copy-start.2 = (f32[16,512,256]{2,1,0:T(8,128)S(1)}, f32[16,512,256]{2,1,0:T(8,128)}, u32[]{:S(2)}) copy-start(f32[16,512,256]{2,1,0:T(8,128)} %copy-done.1) | copy-start | bytes 25165828
  149.7 3.4 %copy-start.3 = (f32[16,512,256]{2,1,0:T(8,128)S(1)}, f32[16,512,256]{2,1,0:T(8,128)}, u32[]{:S(2)}) copy-start(f32[16,512,256]{2,1,0:T(8,128)} %get-tuple-element.8) | copy-start | bytes 25165828
  153.1 46.6 %copy-start.5 = (f32[512,256]{1,0:T(8,128)S(1)}, f32[512,256]{1,0:T(8,128)}, u32[]{:S(2)}) copy-start(f32[512,256]{1,0:T(8,128)} %block_ref.1) | copy-start | bytes 1572868
